TPU v7x, 768 devices: a whole 4x8x12 slice. The times are simulated.
768 devices in a mesh: dp: 96 (over y, z_lo, x), tensor: 8 (over z_hi, core).
Axes of the slice: x: 4, y: 8, z: 12 (z_hi: 4, z_lo: 3; z = z_hi * 3 + z_lo), core: 2. Of those that a mesh axis runs over, the one named last changes fastest.
Arguments:
- inputs: bfloat16 [98304, 8192], P('dp', 'tensor'), may hold values from -6 to 6
- key_weight: bfloat16 [768, 8192], P('dp', 'tensor'), may hold values from -0.0625 to 0.0625
- key_cotangent: bfloat16 [98304, 768], P(('dp', 'tensor')), may hold values from -24 to 24
Outputs:
- key_out: bfloat16 [98304, 768], P(('dp', 'tensor'))
- input_grad: bfloat16 [98304, 8192], P('dp', 'tensor')
- weight_grad: float32 [768, 8192], P('dp', 'tensor')
All inputs are finite; a program needn't handle non-finite values.
Results may differ from a plain program's by a relative error of at most 0.001.
Values may be sent and summed in bfloat16 or wider, within the bound.
A program may use at most 32 MiB of HBM per device.

v0:
```python
import jax
import jax.numpy as jnp
from jax import lax
from jax.sharding import PartitionSpec as P


def body(inputs, key_weight, key_cotangent):
    w_rows = lax.all_gather(key_weight, "dp", axis=0, tiled=True)
    key_out = lax.psum_scatter(
        lax.dot_general(
            inputs, w_rows, (((1,), (1,)), ((), ())), preferred_element_type=jnp.float32
        ),
        "tensor",
        scatter_dimension=0,
        tiled=True,
    ).astype(jnp.bfloat16)
    cot_all = lax.all_gather(key_cotangent, "tensor", axis=0, tiled=True)
    weight_grad = lax.psum_scatter(
        lax.dot_general(
            cot_all, inputs, (((0,), (0,)), ((), ())), preferred_element_type=jnp.float32
        ),
        "dp",
        scatter_dimension=0,
        tiled=True,
    )
    grad_sum = jnp.dot(cot_all, w_rows, preferred_element_type=jnp.float32)
    input_grad = grad_sum.astype(jnp.bfloat16)
    return (key_out, input_grad, weight_grad)


def solution(mesh):
    in_specs = (P("dp", "tensor"), P("dp", "tensor"), P(("dp", "tensor"), None))
    out_specs = (P(("dp", "tensor"), None), P("dp", "tensor"), P("dp", "tensor"))
    return jax.shard_map(body, mesh=mesh, in_specs=in_specs, out_specs=out_specs, check_vma=False)
```

profile of v0, /device:TPU:192, one launch (start us, length us, event | category | flops | bytes accessed | tf_op | source)
XLA Modules:
  0.0 1256.5 jit_solution(7303844079147846382)
XLA Ops:
  7.2 0.0 copy-start
  7.2 0.0 all-gather.3.cloned.1.call-start
  7.2 0.7 all-gather.3.cloned.1.call-update
  7.9 0.0 all-gather.5.cloned.1.call-start
  8.0 0.7 all-gather.5.cloned.1.call-update
  8.7 0.0 reduce-scatter.3.cloned.1.call-start
  8.7 545.7 %all-gather.3.cloned.1.call-done = bf16[768,1024]{1,0:T(8,128)(2,1)} async-done(((bf16[8,1024]{1,0:T(8,128)(2,1)}), bf16[768,1024]{1,0:T(8,128)(2,1)}) %all-gather.3.cloned.1.call-update) | async-done | bytes 1572880 | tf_op jit(solution)/shard_map/all_gather | solution.py:8
  554.4 0.0 copy-done
  554.4 4.9 fusion
  559.3 0.0 reduce-scatter.3.cloned.1.call-update
  559.3 0.0 reduce-scatter.5.cloned.1.call-start
  559.3 37.3 %all-gather.5.cloned.1.call-done = bf16[1024,768]{1,0:T(8,128)(2,1)} async-done(((bf16[128,768]{1,0:T(8,128)(2,1)}), bf16[1024,768]{1,0:T(8,128)(2,1)}) %all-gather.5.cloned.1.call-update) | async-done | bytes 1572880 | tf_op jit(solution)/shard_map/all_gather | solution.py:17
  596.6 4.9 fusion.1
  601.5 0.0 reduce-scatter.5.cloned.1.call-update
  601.5 5.0 convolution_convert_fusion
  606.5 56.0 %reduce-scatter.3.cloned.1.call-done = f32[128,768]{1,0:T(8,128)} async-done(((f32[1024,768]{1,0:T(8,128)}), f32[128,768]{1,0:T(8,128)}) %reduce-scatter.3.cloned.1.call-update) | async-done | bytes 393232 | tf_op jit(solution)/shard_map/reduce_scatter | solution.py:9
  662.5 1.7 convert_element_type.6
  664.2 585.8 %reduce-scatter.5.cloned.1.call-done = f32[8,1024]{1,0:T(8,128)} async-done(((f32[768,1024]{1,0:T(8,128)}), f32[8,1024]{1,0:T(8,128)}) %reduce-scatter.5.cloned.1.call-update) | async-done | bytes 32784 | tf_op jit(solution)/shard_map/reduce_scatter | solution.py:18
Async XLA Ops:
  7.2 547.2 %copy-start = (bf16[1024,1024]{1,0:T(8,128)(2,1)S(1)}, bf16[1024,1024]{1,0:T(8,128)(2,1)}, u32[]{:S(2)}) copy-start(bf16[1024,1024]{1,0:T(8,128)(2,1)} %param.3) | copy-start | bytes 6291460
  7.2 547.2 %all-gather.3.cloned.1.call-start = ((), (), s32[]{:S(2)}) async-start(), calls=%async_computation.2 | async-start | bytes 1589248 | tf_op jit(solution)/shard_map/all_gather | solution.py:8
  7.9 588.7 %all-gather.5.cloned.1.call-start = ((), (), s32[]{:S(2)}) async-start(), calls=%async_computation.4 | async-start | bytes 1769472 | tf_op jit(solution)/shard_map/all_gather | solution.py:17
  8.7 653.8 %reduce-scatter.3.cloned.1.call-start = ((), (), s32[]{:S(2)}) async-start(), calls=%async_computation.3 | async-start | bytes 3538944 | tf_op jit(solution)/shard_map/reduce_scatter | solution.py:9
  559.3 690.6 %reduce-scatter.5.cloned.1.call-start = ((), (), s32[]{:S(2)}) async-start(), calls=%async_computation.5 | async-start | bytes 3178496 | tf_op jit(solution)/shard_map/reduce_scatter | solution.py:18
Sparse Core Ops, SparseCore 0:
  10.4 543.9 all-gather.2
  556.8 39.7 all-gather.4
  599.7 62.6 reduce-scatter.2
  666.0 583.8 reduce-scatter.4
where the time goes:
time: 1260 us
  waiting for transfers between devices  1230 us (98%)
  matrix products  14.8 us (1%)
  between operations  13.8 us (1%)
    reduce_scatter x1, waiting for transfers between devices, body(): lax.psum_scatter(lax.dot_general(cot_all, inputs, (((0,), (0,)), ((), ())...  586 us
    all_gather x1, waiting for transfers between devices, body(): w_rows = lax.all_gather(key_weight, 'dp', axis=0, tiled=True)  546 us
    reduce_scatter x1, waiting for transfers between devices, body(): lax.psum_scatter(lax.dot_general(inputs, w_rows, (((1,), (1,)), ((), ()))...  56 us
    all_gather x1, waiting for transfers between devices, body(): cot_all = lax.all_gather(key_cotangent, 'tensor', axis=0, tiled=True)  37.3 us
  transfers between devices with their start and end apart: 4, of which 4 were waited for; matrix products, arithmetic and copies ran while one was open for 1% of the time, Pallas kernels for 0%

commit v1 on v0

v1 whole, which is shorter than its diff:
```python
import jax
import jax.numpy as jnp
from jax import lax
from jax.experimental import pallas as pl
from jax.experimental.pallas import tpu as pltpu
from jax.sharding import PartitionSpec as P

NX, NY, NL, NH = 4, 8, 3, 4
SUBS_W = 1
SUBS_G = 3
N_COPIES = 160
F32 = jnp.float32
BF16 = jnp.bfloat16


def kernel(
    x_hbm, w_ref, c_hbm,
    key_ref, grad_hbm, wg_ref,
    x_v, wx, wall, cot, part, part_in, key_a, key_b, g, g_half, g_in, gx_in, gz_in, grad_v,
    send_sems, recv_sems, local_sems,
):
    dp = lax.axis_index("dp")
    tn = lax.axis_index("tensor")
    x = dp % NX
    zl = (dp // NX) % NL
    y = dp // (NX * NL)
    core = tn % 2
    zh = tn // 2

    def at(x=x, zl=zl, y=y, zh=zh, core=core):
        return ((y * NL + zl) * NX + x, zh * 2 + core)

    y_up, y_down = (y + 1) % NY, (y + NY - 1) % NY
    h_up, h_down, h_far = (zh + 1) % NH, (zh + NH - 1) % NH, (zh + 2) % NH
    to_yup, to_ydown = at(y=y_up), at(y=y_down)
    to_hup, to_hdown = at(zh=h_up), at(zh=h_down)
    sibling = at(core=1 - core)

    used = [0]
    sends = []

    def send(src, dst, where):
        n = used[0]
        used[0] += 1
        copy = pltpu.make_async_remote_copy(
            src_ref=src, dst_ref=dst, send_sem=send_sems.at[n], recv_sem=recv_sems.at[n],
            device_id=where, device_id_type=pl.DeviceIdType.MESH,
        )
        copy.start()
        sends.append(copy)
        return copy

    load_x = pltpu.make_async_copy(x_hbm, x_v, local_sems.at[0])
    load_x.start()
    load_c = pltpu.make_async_copy(c_hbm, cot.at[tn], local_sems.at[1])
    load_c.start()
    wx[x] = w_ref[...].astype(F32)

    barrier = pltpu.get_barrier_semaphore()
    partners = [at(x=(x + d) % NX) for d in range(1, NX)]
    partners += [at(zl=(zl + d) % NL) for d in range(1, NL)]
    partners += [to_yup, to_ydown, to_hup, to_hdown, sibling]
    for partner in partners:
        pl.semaphore_signal(barrier, inc=1, device_id=partner, device_id_type=pl.DeviceIdType.MESH)
    pl.semaphore_wait(barrier, len(partners))

    w_x = [send(wx.at[x], wx.at[x], at(x=(x + d) % NX)) for d in range(1, NX)]
    load_c.wait()
    c_up = send(cot.at[tn], cot.at[tn], to_hup)
    c_down = send(cot.at[tn], cot.at[tn], to_hdown)
    c_sib = [send(cot.at[tn], cot.at[tn], sibling)]

    for copy in w_x:
        copy.wait_recv()
    mine = y * NL + zl
    wall[mine] = wx[...].reshape(32, 1024).astype(BF16)
    w_z = [send(wall.at[mine], wall.at[mine], at(zl=(zl + d) % NL)) for d in range(1, NL)]
    for copy in w_z:
        copy.wait_recv()

    def w_step(k, q):
        size = NL // SUBS_W
        up = ((y + NY - k) % NY) * NL + q * size
        down = ((y + k) % NY) * NL + q * size
        rows_up, rows_down = (pl.ds(0, 32), pl.ds(0, 32)) if k < 3 else (pl.ds(0, 16), pl.ds(16, 16))
        a = wall.at[pl.ds(up, size), rows_up]
        b = wall.at[pl.ds(down, size), rows_down]
        return send(a, a, to_yup), send(b, b, to_ydown)

    def w_ring(k, before):
        new = []
        for q in range(SUBS_W):
            if before:
                before[q][0].wait_recv()
                before[q][1].wait_recv()
            new.append(w_step(k, q))
        return new

    ring = w_ring(0, None)
    ring = w_ring(1, ring)
    ring = w_ring(2, ring)

    c_up.wait_recv()
    from_down = cot.at[h_down * 2 + core]
    c_far0 = send(from_down.at[pl.ds(0, 64)], from_down.at[pl.ds(0, 64)], to_hup)
    c_down.wait_recv()
    from_up = cot.at[h_up * 2 + core]
    c_far1 = send(from_up.at[pl.ds(64, 64)], from_up.at[pl.ds(64, 64)], to_hdown)
    c_sib.append(send(from_down, from_down, sibling))
    c_sib.append(send(from_up, from_up, sibling))

    ring = w_ring(3, ring)
    load_x.wait()
    for a, b in ring:
        a.wait_recv()
        b.wait_recv()

    s_part = []
    for j, h in enumerate((h_far, h_up, h_down, zh)):
        rows = pl.ds(pl.multiple_of(h * 256, 256), 256)
        prod = lax.dot_general(
            x_v[rows, :], wall[...].reshape(768, 1024), (((1,), (1,)), ((), ())), preferred_element_type=F32
        )
        part[j] = prod.reshape(2, 128, 768)
        s_part.append(send(part.at[j, 1 - core], part_in.at[j], sibling))

    def join(j):
        s_part[j].wait_recv()
        part[j, core] = part[j, core] + part_in[j]

    lo, hi = pl.ds(0, 64), pl.ds(64, 64)
    join(0)
    k_a0 = send(part.at[0, core, lo], key_a.at[0], to_hup)
    k_a1 = send(part.at[0, core, hi], key_a.at[1], to_hdown)
    join(1)
    k_b = [send(part.at[1, core, hi], key_b.at[0, hi], to_hup)]
    join(2)
    k_b.append(send(part.at[2, core, lo], key_b.at[1, lo], to_hdown))

    c_far0.wait_recv()
    c_far1.wait_recv()
    far = cot.at[h_far * 2 + core]
    c_sib.append(send(far, far, sibling))
    join(3)
    for copy in c_sib:
        copy.wait_recv()

    for q in range(3):
        left = cot[:, :, 256 * q : 256 * q + 256].reshape(1024, 256)
        prod = lax.dot_general(left, x_v[...], (((0,), (0,)), ((), ())), preferred_element_type=F32)
        g[8 * q : 8 * q + 8] = prod.reshape(8, 32, 1024)

    size = NL // SUBS_G

    def g_first(q):
        far_y = ((y + 4) % NY) * NL + q * size
        at_q = pl.ds(q * size, size)
        a = send(g.at[pl.ds(far_y, size), pl.ds(0, 16)], g_half.at[0, at_q], to_yup)
        b = send(g.at[pl.ds(far_y, size), pl.ds(16, 16)], g_half.at[1, at_q], to_ydown)
        return a, b

    def g_step(k, q, before):
        at_q = pl.ds(q * size, size)
        up = ((y + 4 - k) % NY) * NL + q * size
        down = ((y + 4 + k) % NY) * NL + q * size
        new = []
        for side, block, where in ((0, up, to_yup), (1, down, to_ydown)):
            before[side].wait_recv()
            here = pl.ds(block, size)
            if k == 1:
                rows = pl.ds(16 * side, 16)
                g[here, rows] = g[here, rows] + g_half[side, at_q]
            else:
                g[here] = g[here] + g_in[side, k - 2, at_q]
            new.append(send(g.at[here], g_in.at[side, k - 1, at_q], where))
        return new

    flow = [g_first(q) for q in range(SUBS_G)]

    def grad_chunk(i):
        prod = jnp.dot(
            cot[2 * i : 2 * i + 2].reshape(256, 768), wall[...].reshape(768, 1024), preferred_element_type=F32
        )
        grad_v[256 * i : 256 * i + 256] = prod.astype(BF16)

    grad_chunk(0)
    grad_chunk(1)
    for q in range(SUBS_G):
        flow[q] = g_step(1, q, flow[q])
    grad_chunk(2)
    grad_chunk(3)
    store_grad = pltpu.make_async_copy(grad_v, grad_hbm, local_sems.at[2])
    store_grad.start()

    k_a0.wait_recv()
    part[1, core, lo] = part[1, core, lo] + key_a[0]
    k_b.append(send(part.at[1, core, lo], key_b.at[0, lo], to_hup))
    k_a1.wait_recv()
    part[2, core, hi] = part[2, core, hi] + key_a[1]
    k_b.append(send(part.at[2, core, hi], key_b.at[1, hi], to_hdown))

    for k in (2, 3):
        for q in range(SUBS_G):
            flow[q] = g_step(k, q, flow[q])
    for q in range(SUBS_G):
        flow[q][0].wait_recv()
        flow[q][1].wait_recv()
    own = pl.ds(y * NL, NL)
    g[own] = g[own] + (g_in[0, 2] + g_in[1, 2])

    g_x = []
    for d in range(1, NX):
        to = (x + d) % NX
        g_x.append(send(g.at[own, pl.ds(pl.multiple_of(to * 8, 8), 8)], gx_in.at[x], at(x=to)))
    gx_in[x] = g[own, pl.ds(pl.multiple_of(x * 8, 8), 8)]
    for copy in g_x:
        copy.wait_recv()
    gz_in[3] = gx_in[0, 0] + gx_in[1, 0] + gx_in[2, 0] + gx_in[3, 0]
    gz_in[4] = gx_in[0, 1] + gx_in[1, 1] + gx_in[2, 1] + gx_in[3, 1]
    gz_in[5] = gx_in[0, 2] + gx_in[1, 2] + gx_in[2, 2] + gx_in[3, 2]
    g_z = []
    for d in range(1, NL):
        to = (zl + d) % NL
        g_z.append(send(gz_in.at[3 + to], gz_in.at[d], at(zl=to)))
    for copy in g_z:
        copy.wait_recv()
    wg_ref[...] = gz_in[3 + zl] + gz_in[1] + gz_in[2]

    for copy in k_b:
        copy.wait_recv()
    key_ref[...] = (part[3, core] + (key_b[0] + key_b[1])).astype(BF16)

    for copy in sends:
        copy.wait_send()
    store_grad.wait()


def body(inputs, key_weight, key_cotangent):
    vmem = pl.BlockSpec(memory_space=pltpu.VMEM)
    hbm = pl.BlockSpec(memory_space=pl.ANY)
    return pl.pallas_call(
        kernel,
        out_shape=(
            jax.ShapeDtypeStruct((128, 768), BF16),
            jax.ShapeDtypeStruct((1024, 1024), BF16),
            jax.ShapeDtypeStruct((8, 1024), F32),
        ),
        in_specs=[hbm, vmem, hbm],
        out_specs=(vmem, hbm, vmem),
        scratch_shapes=[
            pltpu.VMEM((1024, 1024), BF16),
            pltpu.VMEM((NX, 8, 1024), F32),
            pltpu.VMEM((24, 32, 1024), BF16),
            pltpu.VMEM((8, 128, 768), BF16),
            pltpu.VMEM((4, 2, 128, 768), F32),
            pltpu.VMEM((4, 128, 768), F32),
            pltpu.VMEM((2, 64, 768), F32),
            pltpu.VMEM((2, 128, 768), F32),
            pltpu.VMEM((24, 32, 1024), F32),
            pltpu.VMEM((2, 3, 16, 1024), F32),
            pltpu.VMEM((2, 3, 3, 32, 1024), F32),
            pltpu.VMEM((NX, NL, 8, 1024), F32),
            pltpu.VMEM((6, 8, 1024), F32),
            pltpu.VMEM((1024, 1024), BF16),
            pltpu.SemaphoreType.DMA((N_COPIES,)),
            pltpu.SemaphoreType.DMA((N_COPIES,)),
            pltpu.SemaphoreType.DMA((3,)),
        ],
        compiler_params=pltpu.CompilerParams(
            collective_id=0, has_side_effects=True, vmem_limit_bytes=48 * 1024 * 1024
        ),
        cost_estimate=pl.CostEstimate(flops=4_831_838_208, bytes_accessed=5_000_000, transcendentals=0),
    )(inputs, key_weight, key_cotangent)


def solution(mesh):
    in_specs = (P("dp", "tensor"), P("dp", "tensor"), P(("dp", "tensor"), None))
    out_specs = (P(("dp", "tensor"), None), P("dp", "tensor"), P("dp", "tensor"))
    return jax.shard_map(body, mesh=mesh, in_specs=in_specs, out_specs=out_specs, check_vma=False)
```

time: 1260 us -> 128 us (0.10)
  the two profiles are of different devices: /device:TPU:192 before, /device:TPU:4 now
where the time goes in v1:
time: 128 us
  Pallas kernels  122 us (95%)
  local copies, waits for them, and re-layouts  5.84 us (5%)
    pallas_call x1, Pallas kernels, body(): pl.pallas_call(kernel, out_shape=(jax.ShapeDtypeStruct((128, 768), BF16),...  122 us
    unnamed x9, local copies, waits for them, and re-layouts  5.84 us

profile of v1, /device:TPU:4, one launch (start us, length us, event | category | flops | bytes accessed | tf_op | source)
XLA Modules:
  0.0 128.2 jit_solution(2432481437376629934)
XLA Ops:
  0.6 0.0 copy-start
  0.6 1.6 %copy-done = bf16[1024,1024]{1,0:T(8,128)(2,1)S(1)} copy-done((bf16[1024,1024]{1,0:T(8,128)(2,1)S(1)}, bf16[1024,1024]{1,0:T(8,128)(2,1)}, u32[]{:S(2)}) %copy-start) | copy-done | bytes 2097176
  2.2 0.0 copy-start.1
  2.2 0.9 copy-done.1
  3.1 0.0 copy-start.2
  3.2 0.7 copy-done.2
  3.9 121.7 %shard_map.58 = (bf16[128,768]{1,0:T(8,128)(2,1)S(1)}, bf16[1024,1024]{1,0:T(8,128)(2,1)S(1)}, f32[8,1024]{1,0:T(8,128)S(1)}) custom-call(bf16[1024,1024]{1,0:T(8,128)(2,1)S(1)} %copy-done, bf16[8,1024]{1,0:T(8,128)(2,1)S(1)} %copy-done.2, bf16[128,768]{1,0:T(8,128)(2,1)S(1)} %copy-done.1), custom_call_target="tpu_custom_call" | custom-call | flops 4831838208 | bytes 5000000 | tf_op jit(solution)/shard_map/pallas_call | solution.py:241
  125.6 0.7 copy.9
  126.3 1.3 %copy.10 = bf16[1024,1024]{1,0:T(8,128)(2,1)} copy(bf16[1024,1024]{1,0:T(8,128)(2,1)S(1)} %get-tuple-element.7) | data formatting | bytes 4194304
  127.6 0.6 copy.11
Async XLA Ops:
  0.6 1.6 %copy-start = (bf16[1024,1024]{1,0:T(8,128)(2,1)S(1)}, bf16[1024,1024]{1,0:T(8,128)(2,1)}, u32[]{:S(2)}) copy-start(bf16[1024,1024]{1,0:T(8,128)(2,1)} %x_hbm.1) | copy-start | bytes 6291460
  2.2 0.9 copy-start.1
  3.1 0.7 copy-start.2

commit v2 on v1

v2 whole, which is shorter than its diff:
```python
import jax
import jax.numpy as jnp
from jax import lax
from jax.experimental import pallas as pl
from jax.experimental.pallas import tpu as pltpu
from jax.sharding import PartitionSpec as P

NX, NY, NL, NH = 4, 8, 3, 4
SUBS_W = 3
SUBS_G = 3
N_COPIES = 128
VMEM_MIB = 60
F32 = jnp.float32
BF16 = jnp.bfloat16


def kernel(
    x_hbm, w_ref, c_hbm,
    key_ref, grad_hbm, wg_ref,
    x_v, wx, wall, wabs, cot, part, part_in, key_a, key_b, g, a_half, a_in, ax_in, bx_a, bx_in, b_sum, b_half, b_in, gz, grad_v,
    send_sems, recv_sems, local_sems,
):
    dp = lax.axis_index("dp")
    tn = lax.axis_index("tensor")
    x = dp % NX
    zl = (dp // NX) % NL
    y = dp // (NX * NL)
    core = tn % 2
    zh = tn // 2

    def at(x=x, zl=zl, y=y, zh=zh, core=core):
        return ((y * NL + zl) * NX + x, zh * 2 + core)

    y_up, y_down = (y + 1) % NY, (y + NY - 1) % NY
    h_up, h_down, h_far = (zh + 1) % NH, (zh + NH - 1) % NH, (zh + 2) % NH
    to_yup, to_ydown = at(y=y_up), at(y=y_down)
    to_hup, to_hdown = at(zh=h_up), at(zh=h_down)
    sibling = at(core=1 - core)

    used = [0]
    sends = []

    def send(src, dst, where):
        n = used[0]
        used[0] += 1
        copy = pltpu.make_async_remote_copy(
            src_ref=src, dst_ref=dst, send_sem=send_sems.at[n], recv_sem=recv_sems.at[n],
            device_id=where, device_id_type=pl.DeviceIdType.MESH,
        )
        copy.start()
        sends.append(copy)
        return copy

    load_x = pltpu.make_async_copy(x_hbm, x_v, local_sems.at[0])
    load_x.start()
    load_c = pltpu.make_async_copy(c_hbm, cot.at[tn], local_sems.at[1])
    load_c.start()
    wx[x] = w_ref[...].astype(F32)

    barrier = pltpu.get_barrier_semaphore()
    partners = [at(x=(x + d) % NX) for d in range(1, NX)]
    partners += [at(zl=(zl + d) % NL) for d in range(1, NL)]
    partners += [to_yup, to_ydown, to_hup, to_hdown, sibling]
    for partner in partners:
        pl.semaphore_signal(barrier, inc=1, device_id=partner, device_id_type=pl.DeviceIdType.MESH)
    pl.semaphore_wait(barrier, len(partners))

    w_x = [send(wx.at[x], wx.at[x], at(x=(x + d) % NX)) for d in range(1, NX)]
    load_c.wait()
    c_up = send(cot.at[tn], cot.at[tn], to_hup)
    c_down = send(cot.at[tn], cot.at[tn], to_hdown)
    c_sib = [send(cot.at[tn], cot.at[tn], sibling)]

    for copy in w_x:
        copy.wait_recv()
    mine = NL + zl
    wall[mine] = wx[...].reshape(32, 1024).astype(BF16)
    w_z = [send(wall.at[mine], wall.at[mine], at(zl=(zl + d) % NL)) for d in range(1, NL)]
    for copy in w_z:
        copy.wait_recv()

    def w_step(k, q):
        size = NL // SUBS_W
        up, down = (1 - k) % NY, (1 + k) % NY
        rows_up, rows_down = (pl.ds(0, 32), pl.ds(0, 32)) if k < 3 else (pl.ds(0, 16), pl.ds(16, 16))

        def block(place, rows):
            return wall.at[pl.ds(place * NL + q * size, size), rows]

        return (
            send(block(up, rows_up), block((up - 1) % NY, rows_up), to_yup),
            send(block(down, rows_down), block((down + 1) % NY, rows_down), to_ydown),
        )

    def w_ring(k, before):
        new = []
        for q in range(SUBS_W):
            if before:
                before[q][0].wait_recv()
                before[q][1].wait_recv()
            new.append(w_step(k, q))
        return new

    lo, hi = pl.ds(0, 64), pl.ds(64, 64)
    ring = w_ring(0, None)
    ring = w_ring(1, ring)
    ring = w_ring(2, ring)

    c_up.wait_recv()
    from_down = cot.at[h_down * 2 + core]
    c_far0 = send(from_down.at[lo], from_down.at[lo], to_hup)
    c_down.wait_recv()
    from_up = cot.at[h_up * 2 + core]
    c_far1 = send(from_up.at[hi], from_up.at[hi], to_hdown)
    c_sib.append(send(from_down, from_down, sibling))
    c_sib.append(send(from_up, from_up, sibling))

    def key_product(n):
        out = []
        for j, h in enumerate((h_far, h_up, h_down, zh)):
            rows = pl.ds(pl.multiple_of(h * 256, 256), 256)
            prod = lax.dot_general(
                x_v[rows, :], wall[12 * n : 12 * n + 12].reshape(384, 1024), (((1,), (1,)), ((), ())),
                preferred_element_type=F32,
            )
            part[n, j] = prod.reshape(2, 128, 384)
            out.append(send(part.at[n, j, 1 - core], part_in.at[n, j], sibling))
        return out

    def key_first(n, halves):
        def join(j):
            halves[j].wait_recv()
            part[n, j, core] = part[n, j, core] + part_in[n, j]

        join(0)
        a0 = send(part.at[n, 0, core, lo], key_a.at[n, 0], to_hup)
        a1 = send(part.at[n, 0, core, hi], key_a.at[n, 1], to_hdown)
        join(1)
        b = [send(part.at[n, 1, core, hi], key_b.at[n, 0, hi], to_hup)]
        join(2)
        b.append(send(part.at[n, 2, core, lo], key_b.at[n, 1, lo], to_hdown))
        join(3)
        return a0, a1, b

    def key_relay(n, flows):
        a0, a1, b = flows
        a0.wait_recv()
        part[n, 1, core, lo] = part[n, 1, core, lo] + key_a[n, 0]
        b.append(send(part.at[n, 1, core, lo], key_b.at[n, 0, lo], to_hup))
        a1.wait_recv()
        part[n, 2, core, hi] = part[n, 2, core, hi] + key_a[n, 1]
        b.append(send(part.at[n, 2, core, hi], key_b.at[n, 1, hi], to_hdown))
        return b

    load_x.wait()
    halves = key_product(0)
    ring = w_ring(3, ring)
    flows0 = key_first(0, halves)

    for a, b in ring:
        a.wait_recv()
        b.wait_recv()
    halves = key_product(1)

    c_far0.wait_recv()
    c_far1.wait_recv()
    far = cot.at[h_far * 2 + core]
    c_sib.append(send(far, far, sibling))
    flows1 = key_first(1, halves)
    for copy in c_sib:
        copy.wait_recv()

    for q in range(3):
        left = cot[:, :, 256 * q : 256 * q + 256].reshape(1024, 256)
        prod = lax.dot_general(left, x_v[...], (((0,), (0,)), ((), ())), preferred_element_type=F32)
        g[8 * q : 8 * q + 8] = prod.reshape(8, 32, 1024)

    fa, fb = pl.ds(0, 512), pl.ds(512, 512)
    size = NL // SUBS_G

    def a_first(q):
        far_y = ((y + 4) % NY) * NL + q * size
        at_q = pl.ds(q * size, size)
        a = send(g.at[pl.ds(far_y, size), pl.ds(0, 16), fa], a_half.at[0, at_q], to_yup)
        b = send(g.at[pl.ds(far_y, size), pl.ds(16, 16), fa], a_half.at[1, at_q], to_ydown)
        return a, b

    def a_step(k, q, before):
        at_q = pl.ds(q * size, size)
        up = ((y + 4 - k) % NY) * NL + q * size
        down = ((y + 4 + k) % NY) * NL + q * size
        new = []
        for side, block, where in ((0, up, to_yup), (1, down, to_ydown)):
            before[side].wait_recv()
            here = pl.ds(block, size)
            if k == 1:
                rows = pl.ds(16 * side, 16)
                g[here, rows, fa] = g[here, rows, fa] + a_half[side, at_q]
            else:
                g[here, :, fa] = g[here, :, fa] + a_in[side, k - 2, at_q]
            new.append(send(g.at[here, :, fa], a_in.at[side, k - 1, at_q], where))
        return new

    x_up, x_down, x_far = (x + 1) % NX, (x + NX - 1) % NX, (x + 2) % NX
    to_xup, to_xdown = at(x=x_up), at(x=x_down)
    first, last = pl.ds(0, 12), pl.ds(12, 12)

    def rows_of(to):
        return pl.ds(pl.multiple_of(to * 8, 8), 8)

    a_flow = [a_first(q) for q in range(SUBS_G)]
    b_far0 = send(g.at[first, rows_of(x_far), fb], bx_a.at[0], to_xup)
    b_far1 = send(g.at[last, rows_of(x_far), fb], bx_a.at[1], to_xdown)
    b_x = [
        send(g.at[last, rows_of(x_up), fb], bx_in.at[0, last], to_xup),
        send(g.at[first, rows_of(x_down), fb], bx_in.at[1, first], to_xdown),
    ]

    for place in range(NY):
        wabs[pl.ds(((y + NY - 1 + place) % NY) * NL, NL)] = wall[NL * place : NL * place + NL]

    def grad_chunk(i):
        prod = jnp.dot(
            cot[2 * i : 2 * i + 2].reshape(256, 768), wabs[...].reshape(768, 1024), preferred_element_type=F32
        )
        grad_v[256 * i : 256 * i + 256] = prod.astype(BF16)

    grad_chunk(0)
    grad_chunk(1)
    for q in range(SUBS_G):
        a_flow[q] = a_step(1, q, a_flow[q])
    b_far0.wait_recv()
    g[first, rows_of(x_up), fb] = g[first, rows_of(x_up), fb] + bx_a[0]
    b_x.append(send(g.at[first, rows_of(x_up), fb], bx_in.at[0, first], to_xup))
    b_far1.wait_recv()
    g[last, rows_of(x_down), fb] = g[last, rows_of(x_down), fb] + bx_a[1]
    b_x.append(send(g.at[last, rows_of(x_down), fb], bx_in.at[1, last], to_xdown))
    k_b0 = key_relay(0, flows0)
    grad_chunk(2)
    grad_chunk(3)
    store_grad = pltpu.make_async_copy(grad_v, grad_hbm, local_sems.at[2])
    store_grad.start()
    for q in range(SUBS_G):
        a_flow[q] = a_step(2, q, a_flow[q])
    k_b1 = key_relay(1, flows1)

    for copy in b_x:
        copy.wait_recv()
    b_sum[...] = g[:, rows_of(x), fb] + (bx_in[0] + bx_in[1])

    def b_step(k, before):
        new = []
        for side, place, where in ((0, y + 4 - k, to_yup), (1, y + 4 + k, to_ydown)):
            here = pl.ds((place % NY) * NL, NL)
            lanes = pl.ds(256 * side, 256)
            if k > 0:
                before[side].wait_recv()
            if k == 0:
                new.append(send(b_sum.at[here, :, lanes], b_half.at[side], where))
                continue
            if k == 1:
                b_sum[here, :, lanes] = b_sum[here, :, lanes] + b_half[side]
            else:
                b_sum[here] = b_sum[here] + b_in[side, k - 2]
            new.append(send(b_sum.at[here], b_in.at[side, k - 1], where))
        return new

    b_flow = b_step(0, None)
    for q in range(SUBS_G):
        a_flow[q] = a_step(3, q, a_flow[q])
    for k in (1, 2, 3):
        b_flow = b_step(k, b_flow)
    for q in range(SUBS_G):
        a_flow[q][0].wait_recv()
        a_flow[q][1].wait_recv()
    own = pl.ds(y * NL, NL)
    g[own, :, fa] = g[own, :, fa] + (a_in[0, 2] + a_in[1, 2])
    a_x = []
    for d in range(1, NX):
        to = (x + d) % NX
        a_x.append(send(g.at[own, rows_of(to), fa], ax_in.at[x], at(x=to)))
    ax_in[x] = g[own, rows_of(x), fa]
    for copy in b_flow:
        copy.wait_recv()
    gz[pl.ds(3, 3), :, fb] = b_sum[own] + (b_in[0, 2] + b_in[1, 2])
    for copy in a_x:
        copy.wait_recv()
    gz[pl.ds(3, 3), :, fa] = (ax_in[0] + ax_in[1]) + (ax_in[2] + ax_in[3])

    g_z = []
    for d in range(1, NL):
        to = (zl + d) % NL
        g_z.append(send(gz.at[3 + to], gz.at[d], at(zl=to)))

    turn = ((y + NY - 1) % NY) * 96
    gap = lax.broadcasted_iota(jnp.int32, (768, 768), 1) - lax.broadcasted_iota(jnp.int32, (768, 768), 0)
    back = jnp.where((gap == turn) | (gap == turn - 768), 1.0, 0.0).astype(BF16)
    keys = None
    for n, copies in ((0, k_b0), (1, k_b1)):
        for copy in copies:
            copy.wait_recv()
        rel = (part[n, 3, core] + (key_b[n, 0] + key_b[n, 1])).astype(BF16)
        term = jnp.dot(rel, back[384 * n : 384 * n + 384], preferred_element_type=F32)
        keys = term if keys is None else keys + term
    key_ref[...] = keys.astype(BF16)

    for copy in g_z:
        copy.wait_recv()
    wg_ref[...] = gz[3 + zl] + gz[1] + gz[2]

    for copy in sends:
        copy.wait_send()
    store_grad.wait()


def body(inputs, key_weight, key_cotangent):
    vmem = pl.BlockSpec(memory_space=pltpu.VMEM)
    hbm = pl.BlockSpec(memory_space=pl.ANY)
    return pl.pallas_call(
        kernel,
        out_shape=(
            jax.ShapeDtypeStruct((128, 768), BF16),
            jax.ShapeDtypeStruct((1024, 1024), BF16),
            jax.ShapeDtypeStruct((8, 1024), F32),
        ),
        in_specs=[hbm, vmem, hbm],
        out_specs=(vmem, hbm, vmem),
        scratch_shapes=[
            pltpu.VMEM((1024, 1024), BF16),
            pltpu.VMEM((NX, 8, 1024), F32),
            pltpu.VMEM((24, 32, 1024), BF16),
            pltpu.VMEM((24, 32, 1024), BF16),
            pltpu.VMEM((8, 128, 768), BF16),
            pltpu.VMEM((2, 4, 2, 128, 384), F32),
            pltpu.VMEM((2, 4, 128, 384), F32),
            pltpu.VMEM((2, 2, 64, 384), F32),
            pltpu.VMEM((2, 2, 128, 384), F32),
            pltpu.VMEM((24, 32, 1024), F32),
            pltpu.VMEM((2, 3, 16, 512), F32),
            pltpu.VMEM((2, 3, 3, 32, 512), F32),
            pltpu.VMEM((NX, NL, 8, 512), F32),
            pltpu.VMEM((2, 12, 8, 512), F32),
            pltpu.VMEM((2, 24, 8, 512), F32),
            pltpu.VMEM((24, 8, 512), F32),
            pltpu.VMEM((2, 3, 8, 256), F32),
            pltpu.VMEM((2, 3, 3, 8, 512), F32),
            pltpu.VMEM((6, 8, 1024), F32),
            pltpu.VMEM((1024, 1024), BF16),
            pltpu.SemaphoreType.DMA((N_COPIES,)),
            pltpu.SemaphoreType.DMA((N_COPIES,)),
            pltpu.SemaphoreType.DMA((3,)),
        ],
        compiler_params=pltpu.CompilerParams(
            collective_id=0, has_side_effects=True, vmem_limit_bytes=VMEM_MIB * 1024 * 1024
        ),
        cost_estimate=pl.CostEstimate(flops=4_831_838_208, bytes_accessed=5_000_000, transcendentals=0),
    )(inputs, key_weight, key_cotangent)


def solution(mesh):
    in_specs = (P("dp", "tensor"), P("dp", "tensor"), P(("dp", "tensor"), None))
    out_specs = (P(("dp", "tensor"), None), P("dp", "tensor"), P("dp", "tensor"))
    return jax.shard_map(body, mesh=mesh, in_specs=in_specs, out_specs=out_specs, check_vma=False)
```

time: 128 us -> 112 us (0.88)
  the two profiles are of different devices: /device:TPU:4 before, /device:TPU:64 now
where the time goes in v2:
time: 112 us
  Pallas kernels  106 us (95%)
  local copies, waits for them, and re-layouts  5.32 us (5%)
    pallas_call x1, Pallas kernels, body(): pl.pallas_call(kernel, out_shape=(jax.ShapeDtypeStruct((128, 768), BF16),...  106 us
    unnamed x5, local copies, waits for them, and re-layouts  5.32 us

profile of v2, /device:TPU:64, one launch (start us, length us, event | category | flops | bytes accessed | tf_op | source)
XLA Modules:
  0.0 112.0 jit_solution(15948778284886056716)
XLA Ops:
  0.6 106.1 %shard_map.58 = (bf16[128,768]{1,0:T(8,128)(2,1)}, bf16[1024,1024]{1,0:T(8,128)(2,1)}, f32[8,1024]{1,0:T(8,128)}) custom-call(bf16[1024,1024]{1,0:T(8,128)(2,1)} %x_hbm.1, bf16[8,1024]{1,0:T(8,128)(2,1)} %w_ref.1, bf16[128,768]{1,0:T(8,128)(2,1)} %c_hbm.1), custom_call_target="tpu_custom_call" | custom-call | flops 4831838208 | bytes 5000000 | tf_op jit(solution)/shard_map/pallas_call | solution.py:319
  106.7 1.6 %copy.9 = bf16[128,768]{1,0:T(8,128)(2,1)} copy(bf16[128,768]{1,0:T(8,128)(2,1)} %get-tuple-element.6) | data formatting | bytes 393216
  108.3 0.0 copy-start
  108.3 3.1 %copy.10 = bf16[1024,1024]{1,0:T(8,128)(2,1)} copy(bf16[1024,1024]{1,0:T(8,128)(2,1)} %get-tuple-element.7) | data formatting | bytes 4194304
  111.4 0.0 copy-done
  111.4 0.6 copy.11
Async XLA Ops:
  108.3 3.1 %copy-start = (f32[8,1024]{1,0:T(8,128)S(1)}, f32[8,1024]{1,0:T(8,128)}, u32[]{:S(2)}) copy-start(f32[8,1024]{1,0:T(8,128)} %get-tuple-element.8) | copy-start | bytes 98308

commit v3 on v2

--- a/solution.py
+++ b/solution.py
@@ -6,7 +6,6 @@
 from jax.sharding import PartitionSpec as P
 
 NX, NY, NL, NH = 4, 8, 3, 4
-SUBS_W = 3
 SUBS_G = 3
 N_COPIES = 128
 VMEM_MIB = 60
@@ -17,7 +16,7 @@
 def kernel(
     x_hbm, w_ref, c_hbm,
     key_ref, grad_hbm, wg_ref,
-    x_v, wx, wall, wabs, cot, part, part_in, key_a, key_b, g, a_half, a_in, ax_in, bx_a, bx_in, b_sum, b_half, b_in, gz, grad_v,
+    x_v, wz, wa, wb, wall, wabs, cot, part, part_in, key_a, key_b, g, a_half, a_in, ax_in, bx_a, bx_in, b_sum, b_half, b_in, gz, grad_v,
     send_sems, recv_sems, local_sems,
 ):
     dp = lax.axis_index("dp")
@@ -34,6 +33,8 @@
     y_up, y_down = (y + 1) % NY, (y + NY - 1) % NY
     h_up, h_down, h_far = (zh + 1) % NH, (zh + NH - 1) % NH, (zh + 2) % NH
     to_yup, to_ydown = at(y=y_up), at(y=y_down)
+    x_up, x_down, x_far = (x + 1) % NX, (x + NX - 1) % NX, (x + 2) % NX
+    to_xup, to_xdown = at(x=x_up), at(x=x_down)
     to_hup, to_hdown = at(zh=h_up), at(zh=h_down)
     sibling = at(core=1 - core)
 
@@ -55,7 +56,10 @@
     load_x.start()
     load_c = pltpu.make_async_copy(c_hbm, cot.at[tn], local_sems.at[1])
     load_c.start()
-    wx[x] = w_ref[...].astype(F32)
+    w32 = w_ref[...].astype(F32)
+    for half in range(2):
+        quarters = [w32[:, 512 * half + 256 * n : 512 * half + 256 * n + 256] for n in range(2)]
+        wz[zl, half] = jnp.concatenate(quarters, axis=0).astype(BF16)
 
     barrier = pltpu.get_barrier_semaphore()
     partners = [at(x=(x + d) % NX) for d in range(1, NX)]
@@ -65,47 +69,67 @@
         pl.semaphore_signal(barrier, inc=1, device_id=partner, device_id_type=pl.DeviceIdType.MESH)
     pl.semaphore_wait(barrier, len(partners))
 
-    w_x = [send(wx.at[x], wx.at[x], at(x=(x + d) % NX)) for d in range(1, NX)]
+    w_z = [send(wz.at[zl], wz.at[zl], at(zl=(zl + d) % NL)) for d in range(1, NL)]
     load_c.wait()
     c_up = send(cot.at[tn], cot.at[tn], to_hup)
     c_down = send(cot.at[tn], cot.at[tn], to_hdown)
     c_sib = [send(cot.at[tn], cot.at[tn], sibling)]
-
-    for copy in w_x:
-        copy.wait_recv()
-    mine = NL + zl
-    wall[mine] = wx[...].reshape(32, 1024).astype(BF16)
-    w_z = [send(wall.at[mine], wall.at[mine], at(zl=(zl + d) % NL)) for d in range(1, NL)]
     for copy in w_z:
         copy.wait_recv()
 
-    def w_step(k, q):
-        size = NL // SUBS_W
-        up, down = (1 - k) % NY, (1 + k) % NY
-        rows_up, rows_down = (pl.ds(0, 32), pl.ds(0, 32)) if k < 3 else (pl.ds(0, 16), pl.ds(16, 16))
-
-        def block(place, rows):
-            return wall.at[pl.ds(place * NL + q * size, size), rows]
-
-        return (
-            send(block(up, rows_up), block((up - 1) % NY, rows_up), to_yup),
-            send(block(down, rows_down), block((down + 1) % NY, rows_down), to_ydown),
-        )
-
-    def w_ring(k, before):
+    wa[1, x] = wz[:, 0]
+    wa_x = [send(wz.at[:, 0], wa.at[1, x], at(x=(x + d) % NX)) for d in range(1, NX)]
+
+    def wa_step(k, before):
         new = []
-        for q in range(SUBS_W):
+        for q in range(2):
+            for side, place, there, where in ((0, 1 - k, -k, to_yup), (1, 1 + k, 2 + k, to_ydown)):
+                if k == 3 and q != side:
+                    continue
+                if before:
+                    before[2 * q + side].wait_recv()
+                xs = pl.ds(2 * q, 2)
+                new.append(send(wa.at[place % NY, xs], wa.at[there % NY, xs], where))
+        return new
+
+    def wb_step(k, before):
+        new = []
+        for side, place, there, where in ((0, 1 - k, -k, to_yup), (1, 1 + k, 2 + k, to_ydown)):
             if before:
-                before[q][0].wait_recv()
-                before[q][1].wait_recv()
-            new.append(w_step(k, q))
+                before[side].wait_recv()
+            src, dst = (wb.at[x, i % NY] for i in (place, there))
+            if k == 3:
+                lanes = pl.ds(128 * side, 128)
+                src, dst = src.at[:, :, lanes], dst.at[:, :, lanes]
+            new.append(send(src, dst, where))
         return new
 
+    def wb_along_x(n):
+        block = wb.at[x, pl.ds(4 * n, 4)]
+        return send(block, block, to_xup), send(block, block, to_xdown)
+
+    def wait(copies):
+        for copy in copies:
+            copy.wait_recv()
+
+    wb[x, 1] = wz[:, 1]
+    b_ring = wb_step(0, None)
+    b_ring = wb_step(1, b_ring)
+    wait(wa_x)
+    a_ring = wa_step(0, None)
+    wait(b_ring)
+    b_x0 = wb_along_x(0)
+    b_ring = wb_step(2, None)
+    b_ring = wb_step(3, b_ring)
+    a_ring = wa_step(1, a_ring)
+    b_x0[0].wait_recv()
+    block = wb.at[x_down, pl.ds(0, 4)]
+    b_far0 = send(block, block, to_xup)
+    wait(b_ring)
+    b_x1 = wb_along_x(1)
+    a_ring = wa_step(2, a_ring)
+
     lo, hi = pl.ds(0, 64), pl.ds(64, 64)
-    ring = w_ring(0, None)
-    ring = w_ring(1, ring)
-    ring = w_ring(2, ring)
-
     c_up.wait_recv()
     from_down = cot.at[h_down * 2 + core]
     c_far0 = send(from_down.at[lo], from_down.at[lo], to_hup)
@@ -114,6 +138,22 @@
     c_far1 = send(from_up.at[hi], from_up.at[hi], to_hdown)
     c_sib.append(send(from_down, from_down, sibling))
     c_sib.append(send(from_up, from_up, sibling))
+
+    b_x1[1].wait_recv()
+    block = wb.at[x_up, pl.ds(4, 4)]
+    b_far1 = send(block, block, to_xdown)
+    a_last = wa_step(3, a_ring)
+    wait((a_ring[1], a_ring[2]))
+
+    def assemble(n):
+        for place in range(4 * n, 4 * n + 4):
+            for run in range(NL):
+                for half, src in ((0, wa[place, :, run]), (1, wb[:, place, run])):
+                    wide = src.astype(F32)
+                    for quarter in range(2):
+                        rows = wide[:, 8 * quarter : 8 * quarter + 8].reshape(32, 256).astype(BF16)
+                        at_lane = 512 * half + 256 * quarter
+                        wall[place * NL + run, :, at_lane : at_lane + 256] = rows
 
     def key_product(n):
         out = []
@@ -153,13 +193,13 @@
         return b
 
     load_x.wait()
-    halves = key_product(0)
-    ring = w_ring(3, ring)
-    flows0 = key_first(0, halves)
-
-    for a, b in ring:
-        a.wait_recv()
-        b.wait_recv()
+    wait((b_x0[1], b_far0))
+    assemble(0)
+    halves0 = key_product(0)
+    wait((b_x1[0], b_far1))
+    wait(a_last)
+    flows0 = key_first(0, halves0)
+    assemble(1)
     halves = key_product(1)
 
     c_far0.wait_recv()
@@ -201,17 +241,15 @@
             new.append(send(g.at[here, :, fa], a_in.at[side, k - 1, at_q], where))
         return new
 
-    x_up, x_down, x_far = (x + 1) % NX, (x + NX - 1) % NX, (x + 2) % NX
-    to_xup, to_xdown = at(x=x_up), at(x=x_down)
     first, last = pl.ds(0, 12), pl.ds(12, 12)
 
     def rows_of(to):
         return pl.ds(pl.multiple_of(to * 8, 8), 8)
 
     a_flow = [a_first(q) for q in range(SUBS_G)]
-    b_far0 = send(g.at[first, rows_of(x_far), fb], bx_a.at[0], to_xup)
-    b_far1 = send(g.at[last, rows_of(x_far), fb], bx_a.at[1], to_xdown)
-    b_x = [
+    g_far0 = send(g.at[first, rows_of(x_far), fb], bx_a.at[0], to_xup)
+    g_far1 = send(g.at[last, rows_of(x_far), fb], bx_a.at[1], to_xdown)
+    g_x = [
         send(g.at[last, rows_of(x_up), fb], bx_in.at[0, last], to_xup),
         send(g.at[first, rows_of(x_down), fb], bx_in.at[1, first], to_xdown),
     ]
@@ -229,12 +267,12 @@
     grad_chunk(1)
     for q in range(SUBS_G):
         a_flow[q] = a_step(1, q, a_flow[q])
-    b_far0.wait_recv()
+    g_far0.wait_recv()
     g[first, rows_of(x_up), fb] = g[first, rows_of(x_up), fb] + bx_a[0]
-    b_x.append(send(g.at[first, rows_of(x_up), fb], bx_in.at[0, first], to_xup))
-    b_far1.wait_recv()
+    g_x.append(send(g.at[first, rows_of(x_up), fb], bx_in.at[0, first], to_xup))
+    g_far1.wait_recv()
     g[last, rows_of(x_down), fb] = g[last, rows_of(x_down), fb] + bx_a[1]
-    b_x.append(send(g.at[last, rows_of(x_down), fb], bx_in.at[1, last], to_xdown))
+    g_x.append(send(g.at[last, rows_of(x_down), fb], bx_in.at[1, last], to_xdown))
     k_b0 = key_relay(0, flows0)
     grad_chunk(2)
     grad_chunk(3)
@@ -242,9 +280,8 @@
     store_grad.start()
     for q in range(SUBS_G):
         a_flow[q] = a_step(2, q, a_flow[q])
-    k_b1 = key_relay(1, flows1)
-
-    for copy in b_x:
+
+    for copy in g_x:
         copy.wait_recv()
     b_sum[...] = g[:, rows_of(x), fb] + (bx_in[0] + bx_in[1])
 
@@ -268,8 +305,10 @@
     b_flow = b_step(0, None)
     for q in range(SUBS_G):
         a_flow[q] = a_step(3, q, a_flow[q])
-    for k in (1, 2, 3):
-        b_flow = b_step(k, b_flow)
+    b_flow = b_step(1, b_flow)
+    k_b1 = key_relay(1, flows1)
+    b_flow = b_step(2, b_flow)
+    b_flow = b_step(3, b_flow)
     for q in range(SUBS_G):
         a_flow[q][0].wait_recv()
         a_flow[q][1].wait_recv()
@@ -327,7 +366,9 @@
         out_specs=(vmem, hbm, vmem),
         scratch_shapes=[
             pltpu.VMEM((1024, 1024), BF16),
-            pltpu.VMEM((NX, 8, 1024), F32),
+            pltpu.VMEM((NL, 2, 16, 256), BF16),
+            pltpu.VMEM((NY, NX, NL, 16, 256), BF16),
+            pltpu.VMEM((NX, NY, NL, 16, 256), BF16),
             pltpu.VMEM((24, 32, 1024), BF16),
             pltpu.VMEM((24, 32, 1024), BF16),
             pltpu.VMEM((8, 128, 768), BF16),

time: 112 us -> 103 us (0.920)
  the two profiles are of different devices: /device:TPU:64 before, /device:TPU:16 now
where the time goes in v3:
time: 103 us
  Pallas kernels  96.9 us (94%)
  local copies, waits for them, and re-layouts  5.32 us (5%)
    pallas_call x1, Pallas kernels, body(): pl.pallas_call(kernel, out_shape=(jax.ShapeDtypeStruct((128, 768), BF16),...  96.9 us
    unnamed x5, local copies, waits for them, and re-layouts  5.32 us

profile of v3, /device:TPU:16, one launch (start us, length us, event | category | flops | bytes accessed | tf_op | source)
XLA Modules:
  0.0 102.8 jit_solution(2176516637130227607)
XLA Ops:
  0.6 96.9 %shard_map.58 = (bf16[128,768]{1,0:T(8,128)(2,1)}, bf16[1024,1024]{1,0:T(8,128)(2,1)}, f32[8,1024]{1,0:T(8,128)}) custom-call(bf16[1024,1024]{1,0:T(8,128)(2,1)} %x_hbm.1, bf16[8,1024]{1,0:T(8,128)(2,1)} %w_ref.1, bf16[128,768]{1,0:T(8,128)(2,1)} %c_hbm.1), custom_call_target="tpu_custom_call" | custom-call | flops 4831838208 | bytes 5000000 | tf_op jit(solution)/shard_map/pallas_call | solution.py:358
  97.5 1.6 %copy.9 = bf16[128,768]{1,0:T(8,128)(2,1)} copy(bf16[128,768]{1,0:T(8,128)(2,1)} %get-tuple-element.6) | data formatting | bytes 393216
  99.1 0.0 copy-start
  99.1 3.1 %copy.10 = bf16[1024,1024]{1,0:T(8,128)(2,1)} copy(bf16[1024,1024]{1,0:T(8,128)(2,1)} %get-tuple-element.7) | data formatting | bytes 4194304
  102.2 0.0 copy-done
  102.2 0.6 copy.11
Async XLA Ops:
  99.1 3.1 %copy-start = (f32[8,1024]{1,0:T(8,128)S(1)}, f32[8,1024]{1,0:T(8,128)}, u32[]{:S(2)}) copy-start(f32[8,1024]{1,0:T(8,128)} %get-tuple-element.8) | copy-start | bytes 98308

commit v4 on v3

--- a/solution.py
+++ b/solution.py
@@ -195,25 +195,20 @@
     load_x.wait()
     wait((b_x0[1], b_far0))
     assemble(0)
-    halves0 = key_product(0)
-    wait((b_x1[0], b_far1))
-    wait(a_last)
-    flows0 = key_first(0, halves0)
-    assemble(1)
-    halves = key_product(1)
-
+    halves = key_product(0)
     c_far0.wait_recv()
     c_far1.wait_recv()
     far = cot.at[h_far * 2 + core]
     c_sib.append(send(far, far, sibling))
-    flows1 = key_first(1, halves)
-    for copy in c_sib:
-        copy.wait_recv()
-
-    for q in range(3):
-        left = cot[:, :, 256 * q : 256 * q + 256].reshape(1024, 256)
-        prod = lax.dot_general(left, x_v[...], (((0,), (0,)), ((), ())), preferred_element_type=F32)
-        g[8 * q : 8 * q + 8] = prod.reshape(8, 32, 1024)
+    flows0 = key_first(0, halves)
+    wait(c_sib)
+
+    def grad_product(half):
+        lanes = pl.ds(512 * half, 512)
+        for q in range(3):
+            left = cot[:, :, 256 * q : 256 * q + 256].reshape(1024, 256)
+            prod = lax.dot_general(left, x_v[:, lanes], (((0,), (0,)), ((), ())), preferred_element_type=F32)
+            g[8 * q : 8 * q + 8, :, lanes] = prod.reshape(8, 32, 512)
 
     fa, fb = pl.ds(0, 512), pl.ds(512, 512)
     size = NL // SUBS_G
@@ -246,7 +241,7 @@
     def rows_of(to):
         return pl.ds(pl.multiple_of(to * 8, 8), 8)
 
-    a_flow = [a_first(q) for q in range(SUBS_G)]
+    grad_product(1)
     g_far0 = send(g.at[first, rows_of(x_far), fb], bx_a.at[0], to_xup)
     g_far1 = send(g.at[last, rows_of(x_far), fb], bx_a.at[1], to_xdown)
     g_x = [
@@ -254,8 +249,13 @@
         send(g.at[first, rows_of(x_down), fb], bx_in.at[1, first], to_xdown),
     ]
 
-    for place in range(NY):
-        wabs[pl.ds(((y + NY - 1 + place) % NY) * NL, NL)] = wall[NL * place : NL * place + NL]
+    grad_product(0)
+    a_flow = [a_first(q) for q in range(SUBS_G)]
+
+    wait((b_x1[0], b_far1))
+    wait(a_last)
+    assemble(1)
+    flows1 = key_first(1, key_product(1))
 
     def grad_chunk(i):
         prod = jnp.dot(
@@ -263,8 +263,6 @@
         )
         grad_v[256 * i : 256 * i + 256] = prod.astype(BF16)
 
-    grad_chunk(0)
-    grad_chunk(1)
     for q in range(SUBS_G):
         a_flow[q] = a_step(1, q, a_flow[q])
     g_far0.wait_recv()
@@ -274,12 +272,16 @@
     g[last, rows_of(x_down), fb] = g[last, rows_of(x_down), fb] + bx_a[1]
     g_x.append(send(g.at[last, rows_of(x_down), fb], bx_in.at[1, last], to_xdown))
     k_b0 = key_relay(0, flows0)
+    for place in range(NY):
+        wabs[pl.ds(((y + NY - 1 + place) % NY) * NL, NL)] = wall[NL * place : NL * place + NL]
+    grad_chunk(0)
+    grad_chunk(1)
+    for q in range(SUBS_G):
+        a_flow[q] = a_step(2, q, a_flow[q])
     grad_chunk(2)
     grad_chunk(3)
     store_grad = pltpu.make_async_copy(grad_v, grad_hbm, local_sems.at[2])
     store_grad.start()
-    for q in range(SUBS_G):
-        a_flow[q] = a_step(2, q, a_flow[q])
 
     for copy in g_x:
         copy.wait_recv()

time: 103 us -> 105 us (1.019)
  the two profiles are of different devices: /device:TPU:16 before, /device:TPU:64 now
where the time goes in v4:
time: 105 us
  Pallas kernels  99.1 us (94%)
  local copies, waits for them, and re-layouts  5.32 us (5%)
    pallas_call x1, Pallas kernels, body(): pl.pallas_call(kernel, out_shape=(jax.ShapeDtypeStruct((128, 768), BF16),...  99.1 us
    unnamed x5, local copies, waits for them, and re-layouts  5.32 us

profile of v4, /device:TPU:64, one launch (start us, length us, event | category | flops | bytes accessed | tf_op | source)
XLA Modules:
  0.0 105.1 jit_solution(8450717337488744081)
XLA Ops:
  0.6 99.1 %shard_map.58 = (bf16[128,768]{1,0:T(8,128)(2,1)}, bf16[1024,1024]{1,0:T(8,128)(2,1)}, f32[8,1024]{1,0:T(8,128)}) custom-call(bf16[1024,1024]{1,0:T(8,128)(2,1)} %x_hbm.1, bf16[8,1024]{1,0:T(8,128)(2,1)} %w_ref.1, bf16[128,768]{1,0:T(8,128)(2,1)} %c_hbm.1), custom_call_target="tpu_custom_call" | custom-call | flops 4831838208 | bytes 5000000 | tf_op jit(solution)/shard_map/pallas_call | solution.py:360
  99.7 1.6 %copy.9 = bf16[128,768]{1,0:T(8,128)(2,1)} copy(bf16[128,768]{1,0:T(8,128)(2,1)} %get-tuple-element.6) | data formatting | bytes 393216
  101.4 0.0 copy-start
  101.4 3.1 %copy.10 = bf16[1024,1024]{1,0:T(8,128)(2,1)} copy(bf16[1024,1024]{1,0:T(8,128)(2,1)} %get-tuple-element.7) | data formatting | bytes 4194304
  104.4 0.0 copy-done
  104.4 0.6 copy.11
Async XLA Ops:
  101.4 3.1 %copy-start = (f32[8,1024]{1,0:T(8,128)S(1)}, f32[8,1024]{1,0:T(8,128)}, u32[]{:S(2)}) copy-start(f32[8,1024]{1,0:T(8,128)} %get-tuple-element.8) | copy-start | bytes 98308

commit v5 on v3

--- a/solution.py
+++ b/solution.py
@@ -176,11 +176,13 @@
         a0 = send(part.at[n, 0, core, lo], key_a.at[n, 0], to_hup)
         a1 = send(part.at[n, 0, core, hi], key_a.at[n, 1], to_hdown)
         join(1)
-        b = [send(part.at[n, 1, core, hi], key_b.at[n, 0, hi], to_hup)]
         join(2)
-        b.append(send(part.at[n, 2, core, lo], key_b.at[n, 1, lo], to_hdown))
         join(3)
-        return a0, a1, b
+        return a0, a1, []
+
+    def key_own(n, flows):
+        flows[2].append(send(part.at[n, 1, core, hi], key_b.at[n, 0, hi], to_hup))
+        flows[2].append(send(part.at[n, 2, core, lo], key_b.at[n, 1, lo], to_hdown))
 
     def key_relay(n, flows):
         a0, a1, b = flows
@@ -207,6 +209,7 @@
     far = cot.at[h_far * 2 + core]
     c_sib.append(send(far, far, sibling))
     flows1 = key_first(1, halves)
+    key_own(0, flows0)
     for copy in c_sib:
         copy.wait_recv()
 
@@ -274,6 +277,7 @@
     g[last, rows_of(x_down), fb] = g[last, rows_of(x_down), fb] + bx_a[1]
     g_x.append(send(g.at[last, rows_of(x_down), fb], bx_in.at[1, last], to_xdown))
     k_b0 = key_relay(0, flows0)
+    key_own(1, flows1)
     grad_chunk(2)
     grad_chunk(3)
     store_grad = pltpu.make_async_copy(grad_v, grad_hbm, local_sems.at[2])

time: 103 us -> 99.1 us (0.962)
  Pallas kernels: 96.9 us -> 92.9 us
    pallas_call x1, Pallas kernels: 96.9 us -> 92.9 us  [body(): pl.pallas_call(kernel, out_shape=(jax.ShapeDtypeStruct((128, 768), BF16),...]
where the time goes in v5:
time: 99.1 us; the launch traced here: 98.9 us
  Pallas kernels  92.9 us (94%)
  local copies, waits for them, and re-layouts  5.32 us (5%)
    pallas_call x1, Pallas kernels, body(): pl.pallas_call(kernel, out_shape=(jax.ShapeDtypeStruct((128, 768), BF16),...  92.9 us
    unnamed x5, local copies, waits for them, and re-layouts  5.32 us

profile of v5, /device:TPU:16, one launch (start us, length us, event | category | flops | bytes accessed | tf_op | source)
XLA Modules:
  0.0 98.9 jit_solution(7920522259817293788)
XLA Ops:
  0.6 92.9 %shard_map.58 = (bf16[128,768]{1,0:T(8,128)(2,1)}, bf16[1024,1024]{1,0:T(8,128)(2,1)}, f32[8,1024]{1,0:T(8,128)}) custom-call(bf16[1024,1024]{1,0:T(8,128)(2,1)} %x_hbm.1, bf16[8,1024]{1,0:T(8,128)(2,1)} %w_ref.1, bf16[128,768]{1,0:T(8,128)(2,1)} %c_hbm.1), custom_call_target="tpu_custom_call" | custom-call | flops 4831838208 | bytes 5000000 | tf_op jit(solution)/shard_map/pallas_call | solution.py:362
  93.6 1.6 %copy.9 = bf16[128,768]{1,0:T(8,128)(2,1)} copy(bf16[128,768]{1,0:T(8,128)(2,1)} %get-tuple-element.6) | data formatting | bytes 393216
  95.2 0.0 copy-start
  95.2 3.1 %copy.10 = bf16[1024,1024]{1,0:T(8,128)(2,1)} copy(bf16[1024,1024]{1,0:T(8,128)(2,1)} %get-tuple-element.7) | data formatting | bytes 4194304
  98.3 0.0 copy-done
  98.3 0.6 copy.11
Async XLA Ops:
  95.2 3.1 %copy-start = (f32[8,1024]{1,0:T(8,128)S(1)}, f32[8,1024]{1,0:T(8,128)}, u32[]{:S(2)}) copy-start(f32[8,1024]{1,0:T(8,128)} %get-tuple-element.8) | copy-start | bytes 98308
